TPU v7x, 32 devices: a whole 2x2x4 slice. The times are simulated.
32 devices in a mesh: seg: 4 (over y, x), dir: 8 (over z, core).
Axes of the slice: x: 2, y: 2, z: 4, core: 2. Of those that a mesh axis runs over, the one named last changes fastest.
Arguments:
- panel: bfloat16 [16, 45056], P('dir'), may hold values from -6 to 6
- seeds: bfloat16 [4, 16, 45056], P('seg', 'dir'), may hold values from -6 to 6
- inverses: bfloat16 [4, 352, 128, 128], P('seg', 'dir'), may hold values from -1 to 1
- coupling: bfloat16 [4, 3, 128, 128], P('seg'), may hold values from -0.5 to 0.5
- weights: float32 [352, 3], replicated, may hold values from -0.3 to 0.3
- pattern: int32 [352, 3], replicated, may hold values from 0 to 351
- counts: int32 [4], replicated, may hold values from 1 to 2, as said below
Outputs:
- tangent: bfloat16 [4, 16, 45056], P('seg', 'dir')
- adjoint: bfloat16 [4, 16, 45056], P('seg', 'dir')
- projected: float32 [16, 16], P('dir')
Inputs may be any that keep to these rules, and one draw needn't show every extreme that they name: `counts`: some segment takes 2 time steps.
All inputs are finite; a program needn't handle non-finite values.
Results may differ from a plain program's by a relative error of at most 0.019.
Values may be sent and summed in bfloat16 or wider, within the bound.
A program may use at most 64 MiB of HBM per device.

v0:
```python
import math

import jax
import jax.numpy as jnp
from jax import lax
from jax.sharding import PartitionSpec as P

STEPS_MAX = 2


def shifted(array, axis, by):
    size = lax.axis_size(axis)
    pairs = [(i, i + by) for i in range(size) if 0 <= i + by < size]
    return lax.ppermute(array, axis, pairs)


def shifted_2(value, axis, steps):
    count = lax.axis_size(axis)
    pairs = [(source, (source + steps) % count) for source in range(count)]
    return lax.ppermute(value, axis, pairs)


def couple_forward(current, coupling, weights, pattern):
    picked = current[:, pattern, :]
    mixed = (picked.astype(jnp.float32) * weights[None, :, :, None]).astype(jnp.bfloat16)
    pushed = jnp.einsum("rnkb,keb->rne", mixed, coupling, preferred_element_type=jnp.float32)
    return (current.astype(jnp.float32) + pushed).astype(jnp.bfloat16)


def couple_adjoint(reached, coupling, weights, pattern):
    pulled = jnp.einsum(
        "rne,keb->rnkb", reached, coupling, preferred_element_type=jnp.float32
    ).astype(jnp.bfloat16)
    terms = pulled.astype(jnp.float32) * weights[None, :, :, None]
    spread = jnp.zeros(reached.shape, jnp.float32).at[:, pattern, :].add(terms)
    return (reached.astype(jnp.float32) + spread).astype(jnp.bfloat16)


def forward_blocks(current, inverse_table):
    return jnp.einsum(
        "ieq,riq->rie", inverse_table, current, preferred_element_type=jnp.float32
    ).astype(jnp.bfloat16)


def adjoint_blocks(current, inverse_table):
    return jnp.einsum(
        "ieq,rie->riq", inverse_table, current, preferred_element_type=jnp.float32
    ).astype(jnp.bfloat16)


def body(panel, seeds, inverses, coupling, weights, pattern, counts):
    blocks = pattern.shape[0]
    block_width = coupling.shape[-1]
    dir_count = panel.shape[0]
    start_panel = panel.reshape(dir_count, blocks, block_width)
    seed_panel = seeds[0].reshape(dir_count, blocks, block_width)
    inverse_local = inverses[0]
    coupling_here = coupling[0]
    seg_count = lax.axis_size("seg")
    position = lax.axis_index("seg")
    steps_here = counts[position]
    inverse_all = lax.all_gather(inverse_local, "dir", axis=0, tiled=True)

    def diag_forward(current):
        return forward_blocks(current, inverse_all)

    def diag_adjoint(current):
        return adjoint_blocks(current, inverse_all)

    def forward_segment(current):
        for step_index in range(STEPS_MAX):
            advanced = diag_forward(couple_forward(current, coupling_here, weights, pattern))
            current = jnp.where(step_index < steps_here, advanced, current)
        return current

    def adjoint_segment(current):
        for step_index in range(STEPS_MAX):
            advanced = couple_adjoint(diag_adjoint(current), coupling_here, weights, pattern)
            current = jnp.where(step_index < steps_here, advanced, current)
        return current

    def forward_round(round_index, state_pair):
        packet, result = state_pair
        advanced = forward_segment(packet)
        result = jnp.where(position == round_index, advanced, result)
        return (shifted(advanced, "seg", 1), result)

    def adjoint_round(round_index, state_pair):
        packet, result = state_pair
        start_state = (seed_panel.astype(jnp.float32) + packet.astype(jnp.float32)).astype(
            jnp.bfloat16
        )
        advanced = adjoint_segment(start_state)
        active = position == (1 - round_index + seg_count) % seg_count
        result = jnp.where(active, advanced, result)
        return (shifted_2(advanced, "seg", -1), result)

    empty_panel = jnp.zeros_like(start_panel)
    forward_pair = lax.fori_loop(0, seg_count, forward_round, (start_panel, empty_panel))
    adjoint_pair = lax.fori_loop(0, seg_count, adjoint_round, (empty_panel, empty_panel))
    tangent_flat = forward_pair[1].reshape(dir_count, blocks * block_width)
    adjoint_flat = adjoint_pair[1].reshape(dir_count, blocks * block_width)
    rows_tangent, rows_adjoint = (
        lax.all_to_all(tangent_flat, "dir", split_axis=1, concat_axis=0, tiled=True),
        lax.all_to_all(adjoint_flat, "dir", split_axis=1, concat_axis=0, tiled=True),
    )
    scale = 1.0 / math.sqrt(blocks * block_width * seg_count)
    partial_gram = (
        lax.dot_general(
            rows_adjoint, rows_tangent, (((1,), (1,)), ((), ())), preferred_element_type=jnp.float32
        )
        * scale
    )
    own_rows = lax.psum_scatter(partial_gram, "dir", scatter_dimension=0, tiled=True)
    projected = lax.psum(own_rows, "seg")
    return (tangent_flat[None], adjoint_flat[None], projected)


def solution(mesh):
    in_specs = (
        P("dir", None),
        P("seg", "dir", None),
        P("seg", "dir", None, None),
        P("seg", None, None, None),
        P(),
        P(),
        P(),
    )
    out_specs = (P("seg", "dir", None), P("seg", "dir", None), P("dir", None))
    return jax.shard_map(body, mesh=mesh, in_specs=in_specs, out_specs=out_specs, check_vma=False)
```

profile of v0, /device:TPU:0, one launch (start us, length us, event | category | flops | bytes accessed | tf_op | source)
XLA Modules:
  0.0 722.1 jit_solution(1769267488143366211)
XLA Ops:
  10.2 110.3 %all-gather.3.cloned.1.call-done = bf16[1,352,128,128]{3,2,0,1:T(8,128)(2,1)} async-done(((bf16[1,44,128,128]{3,2,0,1:T(8,128)(2,1)}), bf16[1,352,128,128]{3,2,0,1:T(8,128)(2,1)}) %all-gather.3.cloned.1.call-update) | async-done | bytes 11534352 | tf_op jit(solution)/shard_map/all_gather | solution.py:62
  120.5 151.4 %while.36 = (s32[]{:T(128)}, bf16[2,352,128]{2,1,0:T(8,128)(2,1)S(1)}, bf16[2,352,128]{2,1,0:T(8,128)(2,1)S(1)}, pred[]{:T(512)}, pred[]{:T(512)}, /*index=5*/s3...) while((s32[]{:T(128)}, ...), condition=%wide.region_1.2_spmd.clone, body=%wide.region_0.1_spmd.clone.sunk | while | flops 187257952 | bytes 32863540 | solution.py:99
  120.9 4.3 gather_fusion
  125.2 1.4 fusion.61
  126.9 8.8 %fusion.63 = bf16[2,352,128]{2,0,1:T(2,128)(2,1)S(1)} fusion(bf16[352,128,128]{2,1,0:T(8,128)(2,1)} %get-tuple-element.892, pred[]{:T(512)} %get-tuple-element.888, bf16[2,352,128]{2,1,0:T(8,128)(2,1)S(1)} %fusion.62, bf16[2,352,128]{2,1,0:T(8,128)(2,1)S(1)} %get-tuple-element.873), kind=kOutput, calls=%fused_computation.11.clone.1 | convolution fusion | flops 23248896 | bytes 12075009 | tf_op jit(solution)/shard_map/while/body/eval_jaxpr/ieq,riq->rie/dot_general | solution.py:40
  135.7 4.3 gather_fusion.1
  140.0 1.4 fusion.64
  141.7 8.8 %broadcast_select_fusion.10 = (bf16[2,352,128]{2,0,1:T(2,128)(2,1)S(1)}, bf16[2,352,128]{2,0,1:T(2,128)(2,1)S(1)}) fusion(pred[]{:T(512)S(6)} %eq.31, pred[]{:T(512)S(6)} %compare.7, bf16[2,352,128]{2,1,0:T(8,128)(2,1)S(1)} %get-tuple-element.874, bf16[2,352,128]{2,0,1:T(2,128)(2,1)S(1)} %fusion.63, bf16[352,128,128]{2,1,0:T(8,128)(2,1)} %get-tuple-element.892, ...), kind=kOutput, calls=%fused_computation.26.clone.1 | convolution fusion | flops 23699456 | bytes 12615683 | tf_op jit(solution)/shard_map/while/body/eval_jaxpr/ieq,riq->rie/dot_general | solution.py:40
  150.6 3.4 collective-permute-start
  154.0 4.2 collective-permute-done
  158.6 4.3 gather_fusion
  162.9 1.4 fusion.61
  164.6 8.8 %fusion.63 = bf16[2,352,128]{2,0,1:T(2,128)(2,1)S(1)} fusion(bf16[352,128,128]{2,1,0:T(8,128)(2,1)} %get-tuple-element.892, pred[]{:T(512)} %get-tuple-element.888, bf16[2,352,128]{2,1,0:T(8,128)(2,1)S(1)} %fusion.62, bf16[2,352,128]{2,1,0:T(8,128)(2,1)S(1)} %get-tuple-element.873), kind=kOutput, calls=%fused_computation.11.clone.1 | convolution fusion | flops 23248896 | bytes 12075009 | tf_op jit(solution)/shard_map/while/body/eval_jaxpr/ieq,riq->rie/dot_general | solution.py:40
  173.4 4.3 gather_fusion.1
  177.8 1.4 fusion.64
  179.4 8.8 %broadcast_select_fusion.10 = (bf16[2,352,128]{2,0,1:T(2,128)(2,1)S(1)}, bf16[2,352,128]{2,0,1:T(2,128)(2,1)S(1)}) fusion(pred[]{:T(512)S(6)} %eq.31, pred[]{:T(512)S(6)} %compare.7, bf16[2,352,128]{2,1,0:T(8,128)(2,1)S(1)} %get-tuple-element.874, bf16[2,352,128]{2,0,1:T(2,128)(2,1)S(1)} %fusion.63, bf16[352,128,128]{2,1,0:T(8,128)(2,1)} %get-tuple-element.892, ...), kind=kOutput, calls=%fused_computation.26.clone.1 | convolution fusion | flops 23699456 | bytes 12615683 | tf_op jit(solution)/shard_map/while/body/eval_jaxpr/ieq,riq->rie/dot_general | solution.py:40
  188.3 4.4 collective-permute-start
  192.7 3.4 collective-permute-done
  196.5 4.3 gather_fusion
  202.5 8.8 %fusion.63 = bf16[2,352,128]{2,0,1:T(2,128)(2,1)S(1)} fusion(bf16[352,128,128]{2,1,0:T(8,128)(2,1)} %get-tuple-element.892, pred[]{:T(512)} %get-tuple-element.888, bf16[2,352,128]{2,1,0:T(8,128)(2,1)S(1)} %fusion.62, bf16[2,352,128]{2,1,0:T(8,128)(2,1)S(1)} %get-tuple-element.873), kind=kOutput, calls=%fused_computation.11.clone.1 | convolution fusion | flops 23248896 | bytes 12075009 | tf_op jit(solution)/shard_map/while/body/eval_jaxpr/ieq,riq->rie/dot_general | solution.py:40
  211.4 4.3 gather_fusion.1
  217.4 8.8 %broadcast_select_fusion.10 = (bf16[2,352,128]{2,0,1:T(2,128)(2,1)S(1)}, bf16[2,352,128]{2,0,1:T(2,128)(2,1)S(1)}) fusion(pred[]{:T(512)S(6)} %eq.31, pred[]{:T(512)S(6)} %compare.7, bf16[2,352,128]{2,1,0:T(8,128)(2,1)S(1)} %get-tuple-element.874, bf16[2,352,128]{2,0,1:T(2,128)(2,1)S(1)} %fusion.63, bf16[352,128,128]{2,1,0:T(8,128)(2,1)} %get-tuple-element.892, ...), kind=kOutput, calls=%fused_computation.26.clone.1 | convolution fusion | flops 23699456 | bytes 12615683 | tf_op jit(solution)/shard_map/while/body/eval_jaxpr/ieq,riq->rie/dot_general | solution.py:40
  226.2 4.4 collective-permute-start
  230.6 3.0 collective-permute-done
  234.0 4.3 gather_fusion
  240.0 8.8 %fusion.63 = bf16[2,352,128]{2,0,1:T(2,128)(2,1)S(1)} fusion(bf16[352,128,128]{2,1,0:T(8,128)(2,1)} %get-tuple-element.892, pred[]{:T(512)} %get-tuple-element.888, bf16[2,352,128]{2,1,0:T(8,128)(2,1)S(1)} %fusion.62, bf16[2,352,128]{2,1,0:T(8,128)(2,1)S(1)} %get-tuple-element.873), kind=kOutput, calls=%fused_computation.11.clone.1 | convolution fusion | flops 23248896 | bytes 12075009 | tf_op jit(solution)/shard_map/while/body/eval_jaxpr/ieq,riq->rie/dot_general | solution.py:40
  248.9 4.3 gather_fusion.1
  253.2 1.4 fusion.64
  254.9 8.8 %broadcast_select_fusion.10 = (bf16[2,352,128]{2,0,1:T(2,128)(2,1)S(1)}, bf16[2,352,128]{2,0,1:T(2,128)(2,1)S(1)}) fusion(pred[]{:T(512)S(6)} %eq.31, pred[]{:T(512)S(6)} %compare.7, bf16[2,352,128]{2,1,0:T(8,128)(2,1)S(1)} %get-tuple-element.874, bf16[2,352,128]{2,0,1:T(2,128)(2,1)S(1)} %fusion.63, bf16[352,128,128]{2,1,0:T(8,128)(2,1)} %get-tuple-element.892, ...), kind=kOutput, calls=%fused_computation.26.clone.1 | convolution fusion | flops 23699456 | bytes 12615683 | tf_op jit(solution)/shard_map/while/body/eval_jaxpr/ieq,riq->rie/dot_general | solution.py:40
  263.7 5.2 collective-permute-start
  268.9 3.0 collective-permute-done
  273.0 3.6 all-to-all-start.1
  276.7 399.9 %while.37 = (s32[]{:T(128)}, bf16[2,352,128]{2,0,1:T(2,128)(2,1)S(1)}, bf16[2,352,128]{2,0,1:T(2,128)(2,1)}, pred[]{:T(512)}, pred[]{:T(512)}, /*index=5*/bf16[2...) while((s32[]{:T(128)}, ...), condition=%wide.region_5.6_spmd.clone, body=%wide.region_2.5_spmd.clone.sunk | while | flops 188337264 | bytes 40961356 | solution.py:100
  276.7 5.9 bitcast_convert_fusion.4
  284.0 38.2 %scatter_fusion = f32[2,352,128]{2,0,1:T(2,128)S(1)} fusion(f32[2,352,128]{2,0,1:T(2,128)S(1)} %get-tuple-element.854, s32[1056]{0:T(1024)S(1)} %reshape.146, f32[1056,2,128]{2,1,0:T(2,128)S(1)} %bitcast.134), kind=kCustom, calls=%fused_computation.2.clone.clone.1 | custom fusion | flops 270336 | bytes 3248256 | tf_op jit(solution)/shard_map/while/body/eval_jaxpr/scatter-add | solution.py:35
  322.5 5.9 bitcast_convert_fusion.5
  329.6 38.2 %scatter_fusion.1 = f32[2,352,128]{2,0,1:T(2,128)S(1)} fusion(f32[2,352,128]{2,0,1:T(2,128)S(1)} %get-tuple-element.856, s32[1056]{0:T(1024)S(1)} %reshape.146, f32[1056,2,128]{2,1,0:T(2,128)S(1)} %bitcast.133), kind=kCustom, calls=%fused_computation.3.clone.clone.1 | custom fusion | flops 270336 | bytes 3248256 | tf_op jit(solution)/shard_map/while/body/eval_jaxpr/scatter-add | solution.py:35
  368.9 3.9 collective-permute-start.1
  372.7 4.5 collective-permute-done.1
  377.2 5.9 bitcast_convert_fusion.4
  384.5 38.2 %scatter_fusion = f32[2,352,128]{2,0,1:T(2,128)S(1)} fusion(f32[2,352,128]{2,0,1:T(2,128)S(1)} %get-tuple-element.854, s32[1056]{0:T(1024)S(1)} %reshape.146, f32[1056,2,128]{2,1,0:T(2,128)S(1)} %bitcast.134), kind=kCustom, calls=%fused_computation.2.clone.clone.1 | custom fusion | flops 270336 | bytes 3248256 | tf_op jit(solution)/shard_map/while/body/eval_jaxpr/scatter-add | solution.py:35
  422.9 5.9 bitcast_convert_fusion.5
  430.1 38.2 %scatter_fusion.1 = f32[2,352,128]{2,0,1:T(2,128)S(1)} fusion(f32[2,352,128]{2,0,1:T(2,128)S(1)} %get-tuple-element.856, s32[1056]{0:T(1024)S(1)} %reshape.146, f32[1056,2,128]{2,1,0:T(2,128)S(1)} %bitcast.133), kind=kCustom, calls=%fused_computation.3.clone.clone.1 | custom fusion | flops 270336 | bytes 3248256 | tf_op jit(solution)/shard_map/while/body/eval_jaxpr/scatter-add | solution.py:35
  468.3 1.9 broadcast_select_fusion.12
  470.2 3.1 collective-permute-start.1
  473.3 4.7 collective-permute-done.1
  478.0 5.9 bitcast_convert_fusion.4
  485.4 38.2 %scatter_fusion = f32[2,352,128]{2,0,1:T(2,128)S(1)} fusion(f32[2,352,128]{2,0,1:T(2,128)S(1)} %get-tuple-element.854, s32[1056]{0:T(1024)S(1)} %reshape.146, f32[1056,2,128]{2,1,0:T(2,128)S(1)} %bitcast.134), kind=kCustom, calls=%fused_computation.2.clone.clone.1 | custom fusion | flops 270336 | bytes 3248256 | tf_op jit(solution)/shard_map/while/body/eval_jaxpr/scatter-add | solution.py:35
  523.8 5.9 bitcast_convert_fusion.5
  530.9 38.2 %scatter_fusion.1 = f32[2,352,128]{2,0,1:T(2,128)S(1)} fusion(f32[2,352,128]{2,0,1:T(2,128)S(1)} %get-tuple-element.856, s32[1056]{0:T(1024)S(1)} %reshape.146, f32[1056,2,128]{2,1,0:T(2,128)S(1)} %bitcast.133), kind=kCustom, calls=%fused_computation.3.clone.clone.1 | custom fusion | flops 270336 | bytes 3248256 | tf_op jit(solution)/shard_map/while/body/eval_jaxpr/scatter-add | solution.py:35
  569.1 1.9 broadcast_select_fusion.12
  571.1 2.0 collective-permute-start.1
  573.1 4.2 collective-permute-done.1
  577.3 5.9 bitcast_convert_fusion.4
  584.6 38.2 %scatter_fusion = f32[2,352,128]{2,0,1:T(2,128)S(1)} fusion(f32[2,352,128]{2,0,1:T(2,128)S(1)} %get-tuple-element.854, s32[1056]{0:T(1024)S(1)} %reshape.146, f32[1056,2,128]{2,1,0:T(2,128)S(1)} %bitcast.134), kind=kCustom, calls=%fused_computation.2.clone.clone.1 | custom fusion | flops 270336 | bytes 3248256 | tf_op jit(solution)/shard_map/while/body/eval_jaxpr/scatter-add | solution.py:35
  623.0 5.9 bitcast_convert_fusion.5
  630.2 38.2 %scatter_fusion.1 = f32[2,352,128]{2,0,1:T(2,128)S(1)} fusion(f32[2,352,128]{2,0,1:T(2,128)S(1)} %get-tuple-element.856, s32[1056]{0:T(1024)S(1)} %reshape.146, f32[1056,2,128]{2,1,0:T(2,128)S(1)} %bitcast.133), kind=kCustom, calls=%fused_computation.3.clone.clone.1 | custom fusion | flops 270336 | bytes 3248256 | tf_op jit(solution)/shard_map/while/body/eval_jaxpr/scatter-add | solution.py:35
  668.4 1.9 broadcast_select_fusion.12
  670.3 2.2 collective-permute-start.1
  672.5 4.1 collective-permute-done.1
  676.6 4.6 all-to-all-start
  683.3 6.0 all-to-all-done
  689.5 14.8 %all-reduce = f32[16,16]{1,0:T(8,128)S(1)} all-reduce(f32[16,16]{1,0:T(8,128)S(1)} %convolution_multiply_fusion), channel_id=3, replica_groups=mesh['seg'=4,'dir'=8] {'dir'}, use_global_device_ids=true, to_apply=%region_6.7.clone | all-reduce | flops 256 | bytes 2048
  704.3 10.9 %psum.7 = f32[2,16]{1,0:T(2,128)} all-reduce(f32[2,16]{1,0:T(2,128)S(1)} %constant_dynamic-slice_fusion), channel_id=1, replica_groups=mesh['seg'=4,'dir'=8] {'seg'}, use_global_device_ids=true, to_apply=%region_7.8 | all-reduce | flops 32 | bytes 256 | tf_op jit(solution)/shard_map/psum | solution.py:115
  (96 shorter events, 24.7 us)
Async XLA Ops:
  7.2 0.8 copy-start.5
  7.2 2.7 copy-start.4
  7.2 2.8 copy-start.3
  7.2 2.9 copy-start.2
  7.2 113.3 %all-gather.3.cloned.1.call-start = ((), (), s32[]{:S(2)}) async-start(), calls=%async_computation.2 | async-start | bytes 12976128 | tf_op jit(solution)/shard_map/all_gather | solution.py:62
  7.3 113.2 %copy-start.1 = (bf16[1,3,128,128]{3,2,1,0:T(8,128)(2,1)S(1)}, bf16[1,3,128,128]{3,2,1,0:T(8,128)(2,1)}, u32[]{:S(2)}) copy-start(bf16[1,3,128,128]{3,2,1,0:T(8,128)(2,1)} %param.14) | copy-start | bytes 294916
  150.6 7.6 %collective-permute-start = (bf16[2,352,128]{2,0,1:T(2,128)(2,1)S(1)}, bf16[2,352,128]{2,0,1:T(2,128)(2,1)S(1)}, u32[]{:S(2)}, u32[]{:S(2)}) collective-permute-start(bf16[2,352,128]{2,0,1:T(2,128)(2,1)S(1)} %get-tuple-element.841), channel_id=1, source_target_pairs={{0,8},{8,16},{16,24},{1,9},{9,17},{17,25},{2,10},{10,18},{18,26},{... | collective-permute-start | bytes 540680 | tf_op jit(solution)/shard_map/while/body/eval_jaxpr/ppermute | solution.py:14
  188.3 7.8 %collective-permute-start = (bf16[2,352,128]{2,0,1:T(2,128)(2,1)S(1)}, bf16[2,352,128]{2,0,1:T(2,128)(2,1)S(1)}, u32[]{:S(2)}, u32[]{:S(2)}) collective-permute-start(bf16[2,352,128]{2,0,1:T(2,128)(2,1)S(1)} %get-tuple-element.841), channel_id=1, source_target_pairs={{0,8},{8,16},{16,24},{1,9},{9,17},{17,25},{2,10},{10,18},{18,26},{... | collective-permute-start | bytes 540680 | tf_op jit(solution)/shard_map/while/body/eval_jaxpr/ppermute | solution.py:14
  226.2 7.4 %collective-permute-start = (bf16[2,352,128]{2,0,1:T(2,128)(2,1)S(1)}, bf16[2,352,128]{2,0,1:T(2,128)(2,1)S(1)}, u32[]{:S(2)}, u32[]{:S(2)}) collective-permute-start(bf16[2,352,128]{2,0,1:T(2,128)(2,1)S(1)} %get-tuple-element.841), channel_id=1, source_target_pairs={{0,8},{8,16},{16,24},{1,9},{9,17},{17,25},{2,10},{10,18},{18,26},{... | collective-permute-start | bytes 540680 | tf_op jit(solution)/shard_map/while/body/eval_jaxpr/ppermute | solution.py:14
  263.7 8.2 %collective-permute-start = (bf16[2,352,128]{2,0,1:T(2,128)(2,1)S(1)}, bf16[2,352,128]{2,0,1:T(2,128)(2,1)S(1)}, u32[]{:S(2)}, u32[]{:S(2)}) collective-permute-start(bf16[2,352,128]{2,0,1:T(2,128)(2,1)S(1)} %get-tuple-element.841), channel_id=1, source_target_pairs={{0,8},{8,16},{16,24},{1,9},{9,17},{17,25},{2,10},{10,18},{18,26},{... | collective-permute-start | bytes 540680 | tf_op jit(solution)/shard_map/while/body/eval_jaxpr/ppermute | solution.py:14
  271.9 4.7 copy-start
  273.0 403.6 %all-to-all-start.1 = ((bf16[2,8,5632]{2,0,1:T(2,128)(2,1)}), bf16[2,8,5632]{2,0,1:T(2,128)(2,1)S(1)}, u32[]{:S(2)}, u32[]{:S(2)}) async-start(bf16[2,8,5632]{2,0,1:T(2,128)(2,1)} %copy.90), calls=%async_computation.1 | async-start | bytes 360448 | tf_op jit(solution)/shard_map/all_to_all | solution.py:104
  276.7 404.6 %copy-start.6 = (u32[32]{0:T(128)S(1)}, u32[32]{0:T(128)}, u32[]{:S(2)}) copy-start(u32[32]{0:T(128)} %constant.117) | copy-start | bytes 388
  368.9 8.3 %collective-permute-start.1 = (bf16[2,352,128]{2,0,1:T(2,128)(2,1)S(1)}, bf16[2,352,128]{2,0,1:T(2,128)(2,1)S(1)}, u32[]{:S(2)}, u32[]{:S(2)}) collective-permute-start(bf16[2,352,128]{2,0,1:T(2,128)(2,1)S(1)} %get-tuple-element.858), channel_id=1, source_target_pairs={{0,24},{8,0},{16,8},{24,16},{1,25},{9,1},{17,9},{25,17},{2,26},{10... | collective-permute-start | bytes 540680 | tf_op jit(solution)/shard_map/while/body/eval_jaxpr/ppermute | solution.py:20
  470.2 7.8 %collective-permute-start.1 = (bf16[2,352,128]{2,0,1:T(2,128)(2,1)S(1)}, bf16[2,352,128]{2,0,1:T(2,128)(2,1)S(1)}, u32[]{:S(2)}, u32[]{:S(2)}) collective-permute-start(bf16[2,352,128]{2,0,1:T(2,128)(2,1)S(1)} %get-tuple-element.858), channel_id=1, source_target_pairs={{0,24},{8,0},{16,8},{24,16},{1,25},{9,1},{17,9},{25,17},{2,26},{10... | collective-permute-start | bytes 540680 | tf_op jit(solution)/shard_map/while/body/eval_jaxpr/ppermute | solution.py:20
  571.1 6.2 collective-permute-start.1
  670.3 6.3 collective-permute-start.1
  676.6 12.6 %all-to-all-start = ((bf16[2,8,5632]{2,0,1:T(2,128)(2,1)}), bf16[2,8,5632]{2,0,1:T(2,128)(2,1)S(1)}, u32[]{:S(2)}, u32[]{:S(2)}) async-start(bf16[2,8,5632]{2,0,1:T(2,128)(2,1)} %bitcast.7), calls=%async_computation | async-start | bytes 360448 | tf_op jit(solution)/shard_map/all_to_all | solution.py:105
Sparse Core Ops, SparseCore 0:
  9.7 110.7 all-gather.2
where the time goes:
time: 723 us; the launch traced here: 722 us
  other arithmetic  325 us (45%)
  waiting for transfers between devices  148 us (20%)
  matrix products  123 us (17%)
  local copies, waits for them, and re-layouts  47 us (7%)
  starting transfers between devices  36.8 us (5%)
  blocking collectives  25.7 us (4%)
  between operations  16.2 us (2%)
    scatter-add x8, other arithmetic, couple_adjoint(): spread = jnp.zeros(reached.shape, jnp.float32).at[:, pattern, :].add(terms)  306 us
    all_gather x1, waiting for transfers between devices, body(): inverse_all = lax.all_gather(inverse_local, 'dir', axis=0, tiled=True)  110 us
    dot_general x8, matrix products, forward_blocks(): jnp.einsum('ieq,riq->rie', inverse_table, current, preferred_element_type...  70.7 us
    dot_general x8, matrix products, adjoint_blocks(): jnp.einsum('ieq,rie->riq', inverse_table, current, preferred_element_type...  47.5 us
    gather x8, local copies, waits for them, and re-layouts, couple_forward(): picked = current[:, pattern, :]  34.4 us
    ppermute x4, waiting for transfers between devices, shifted_2(): return lax.ppermute(value, axis, pairs)  17.4 us
    ppermute x4, starting transfers between devices, shifted(): return lax.ppermute(array, axis, pairs)  17.4 us
    unnamed x1, blocking collectives  14.8 us
  transfers between devices with their start and end apart: 11, of which 10 were waited for; matrix products, arithmetic and copies ran while one was open for 52% of the time, Pallas kernels for 0%

commit v1 on v0

v1 whole, which is shorter than its diff:
```python
import functools
import math

import jax
import jax.numpy as jnp
from jax import lax
from jax.experimental import pallas as pl
from jax.experimental.pallas import tpu as pltpu
from jax.sharding import PartitionSpec as P

MESH = pl.DeviceIdType.MESH
F32 = jnp.float32
BF16 = jnp.bfloat16

SEED, F1, F2, F3, TAN, HAND_F, HAND_G, G2, G3, G4, ADJ = range(11)
EXCHANGES = 11


def kernel(
    dims,
    panel_ref, seeds_ref, inv_ref, cf_ref, cg_ref, wf_ref, wg_ref, counts_ref,
    tangent_ref, adjoint_ref, proj_ref,
    land, f1s, f2s, f3s, tans, g2s, g3s, g4s, adjs, ubuf, obuf, pbuf, rp, qbuf, rq,
    send_sem, recv_sem, ps_sem, pr_sem, qs_sem, qr_sem,
):
    S, D, R, nb, pb, B, K, scale = dims
    N = D * pb
    rows = D * R
    s = lax.axis_index("seg")
    d = lax.axis_index("dir")

    barrier = pltpu.get_barrier_semaphore()
    total = S * D
    lin = s * D + d

    def greet(o, c):
        t = lax.rem(lin + o, total)
        pl.semaphore_signal(
            barrier, inc=1, device_id=(lax.div(t, D), lax.rem(t, D)), device_id_type=MESH
        )
        return c

    lax.fori_loop(1, total, greet, 0)
    pl.semaphore_wait(barrier, total - 1)

    ubuf[...] = jnp.zeros_like(ubuf)
    obuf[...] = jnp.zeros_like(obuf)

    def copy(src, ex, seg, to, came_from):
        return pltpu.make_async_remote_copy(
            src_ref=src.at[to],
            dst_ref=land.at[ex, came_from],
            send_sem=send_sem.at[ex, to],
            recv_sem=recv_sem.at[ex, came_from],
            device_id=(seg, to),
            device_id_type=MESH,
        )

    def send_group(src, ex):
        def one(o, c):
            copy(src, ex, s, lax.rem(d + o, D), d).start()
            return c

        lax.fori_loop(1, D, one, 0)
        land[ex, d] = src[d]

    def wait_group(src, ex):
        def one(o, c):
            j = lax.rem(d + D - o, D)
            copy(src, ex, s, j, j).wait_recv()
            return c

        lax.fori_loop(1, D, one, 0)

    def sent_group(src, ex):
        def one(o, c):
            copy(src, ex, s, lax.rem(d + o, D), d).wait_send()
            return c

        lax.fori_loop(1, D, one, 0)

    def send_on(src, ex, seg):
        def one(o, c):
            copy(src, ex, seg, lax.rem(d + o, D), d).start()
            return c

        lax.fori_loop(0, D, one, 0)

    def wait_on(src, ex, seg):
        def one(o, c):
            copy(src, ex, seg, o, o).wait_recv()
            return c

        lax.fori_loop(0, D, one, 0)

    def sent_on(src, ex, seg):
        def one(o, c):
            copy(src, ex, seg, o, d).wait_send()
            return c

        lax.fori_loop(0, D, one, 0)

    def couple(x, w_ref, c_ref):
        parts = [jnp.dot(v, c_ref[...], preferred_element_type=F32).astype(BF16) for v in x]
        rhs = jnp.concatenate(
            [
                jnp.concatenate([p[:, k * B : (k + 1) * B] for p in parts], axis=1)
                for k in range(K)
            ],
            axis=0,
        )
        acc = jnp.dot(w_ref[...], rhs, preferred_element_type=F32)
        return [x[r].astype(F32) + acc[:, r * B : (r + 1) * B] for r in range(R)]

    def split(value):
        return [value[:, r].reshape(N, B) for r in range(R)]

    def put(ref, parts):
        for r in range(R):
            ref[:, r] = parts[r].astype(BF16).reshape(D, pb, B)

    group = max(g for g in range(1, 17) if nb % g == 0)

    def invert(value, contract):
        ubuf[...] = value.astype(F32).reshape(rows * pb, B)

        def step(g, c):
            for u in range(group):
                at = pl.ds(g * group + u, rows, stride=pb)
                obuf[at, :] = lax.dot_general(
                    ubuf[at, :].astype(BF16),
                    inv_ref[g * group + u],
                    (((1,), (contract,)), ((), ())),
                    preferred_element_type=F32,
                )
            return c

        lax.fori_loop(0, nb // group, step, 0)
        return obuf[...].astype(BF16).reshape(D, R, pb, B)

    send_group(seeds_ref, SEED)
    more = counts_ref[s] > 1

    def tangent_round():
        @pl.when(s > 0)
        def _():
            wait_on(tans, HAND_F, s)

        first = jnp.where(s > 0, land[HAND_F], panel_ref[...])
        put(f1s, couple(split(first), wf_ref, cf_ref))
        send_group(f1s, F1)
        wait_group(f1s, F1)
        f2s[...] = invert(land[F1], 1)
        send_group(f2s, F2)
        wait_group(f2s, F2)
        put(f3s, couple(split(land[F2]), wf_ref, cf_ref))
        send_group(f3s, F3)
        wait_group(f3s, F3)
        tans[...] = jnp.where(more, invert(land[F3], 1), f2s[...])

        @pl.when(s < S - 1)
        def _():
            send_on(tans, HAND_F, lax.rem(s + 1, S))

        send_group(tans, TAN)

    def adjoint_round():
        wait_group(seeds_ref, SEED)

        @pl.when(s != 1)
        def _():
            wait_on(adjs, HAND_G, s)

        entry = jnp.where(
            s != 1,
            (land[SEED].astype(F32) + land[HAND_G].astype(F32)).astype(BF16),
            land[SEED],
        )
        g2s[...] = invert(entry, 0)
        send_group(g2s, G2)
        wait_group(g2s, G2)
        put(g3s, couple(split(land[G2]), wg_ref, cg_ref))
        send_group(g3s, G3)
        wait_group(g3s, G3)
        g4s[...] = invert(land[G3], 0)
        send_group(g4s, G4)
        wait_group(g4s, G4)
        done = couple(split(land[G4]), wg_ref, cg_ref)
        put(adjs, done)
        adjs[...] = jnp.where(more, adjs[...], g3s[...])

        @pl.when(s != 2)
        def _():
            send_on(adjs, HAND_G, lax.rem(s + S - 1, S))

        send_group(adjs, ADJ)

    tangent_first = s < lax.rem(1 - s + S, S)

    def turn(slot, c):
        now = (slot == 0) == tangent_first

        @pl.when(now)
        def _():
            tangent_round()

        @pl.when(jnp.logical_not(now))
        def _():
            adjoint_round()

        return c

    lax.fori_loop(0, 2, turn, 0)

    adjoint_ref[...] = adjs[...]
    wait_group(adjs, ADJ)
    ubuf[...] = land[ADJ].astype(F32).reshape(rows * pb, B)
    obuf[...] = tans[...].astype(F32).reshape(rows * pb, B)

    def gram(g, acc):
        spots = [pl.ds(g * group + u, rows, stride=pb) for u in range(group)]
        left = jnp.concatenate([ubuf[at, :].astype(BF16) for at in spots], axis=1)
        right = jnp.concatenate([obuf[at, :].astype(BF16) for at in spots], axis=1)
        return acc + lax.dot_general(
            left, right, (((1,), (1,)), ((), ())), preferred_element_type=F32
        )

    pbuf[...] = jnp.zeros_like(pbuf)
    pbuf[:, 0:rows] = lax.fori_loop(0, nb // group, gram, jnp.zeros((rows, rows), F32))

    def pcopy(to, came_from):
        return pltpu.make_async_remote_copy(
            src_ref=pbuf, dst_ref=rp.at[came_from], send_sem=ps_sem.at[to],
            recv_sem=pr_sem.at[came_from], device_id=(s, to), device_id_type=MESH,
        )

    def qcopy(to, came_from):
        return pltpu.make_async_remote_copy(
            src_ref=qbuf, dst_ref=rq.at[came_from], send_sem=qs_sem.at[to],
            recv_sem=qr_sem.at[came_from], device_id=(to, d), device_id_type=MESH,
        )

    rp[d] = pbuf[...]
    for o in range(1, D):
        pcopy(lax.rem(d + o, D), d).start()
    for o in range(1, D):
        j = lax.rem(d + D - o, D)
        pcopy(j, j).wait_recv()
    qbuf[...] = jnp.sum(rp[...], axis=0)
    rq[s] = qbuf[...]
    for o in range(1, S):
        qcopy(lax.rem(s + o, S), s).start()
    wait_group(tans, TAN)
    tangent_ref[...] = land[TAN]
    for o in range(1, S):
        j = lax.rem(s + S - o, S)
        qcopy(j, j).wait_recv()
    for o in range(1, D):
        pcopy(lax.rem(d + o, D), d).wait_send()
    pbuf[...] = jnp.sum(rq[...], axis=0) * scale
    proj_ref[...] = pbuf[pl.ds(d * R, R), :]

    for o in range(1, S):
        qcopy(lax.rem(s + o, S), s).wait_send()
    for src, ex in (
        (seeds_ref, SEED), (f1s, F1), (f2s, F2), (f3s, F3), (tans, TAN),
        (g2s, G2), (g3s, G3), (g4s, G4), (adjs, ADJ),
    ):
        sent_group(src, ex)

    @pl.when(s < S - 1)
    def _():
        sent_on(tans, HAND_F, lax.rem(s + 1, S))

    @pl.when(s != 2)
    def _():
        sent_on(adjs, HAND_G, lax.rem(s + S - 1, S))


def body(panel, seeds, inverses, coupling, weights, pattern, counts):
    NB, K = pattern.shape
    B = coupling.shape[-1]
    R = panel.shape[0]
    S, D = lax.axis_size("seg"), lax.axis_size("dir")
    nb = NB // D
    pb = -(-nb // 16) * 16
    N = D * pb
    rows = D * R

    def padded(flat):
        cut = flat.reshape(R, D, nb, B).transpose(1, 0, 2, 3)
        return jnp.pad(cut, ((0, 0), (0, 0), (0, pb - nb), (0, 0)))

    def flat(cut):
        return cut[:, :, :nb].transpose(1, 0, 2, 3).reshape(R, NB * B)

    place = (pattern // nb) * pb + pattern % nb
    place = jnp.pad(place.reshape(D, nb, K), ((0, 0), (0, pb - nb), (0, 0)), constant_values=-1)
    place = place.reshape(N, K)
    factor = jnp.pad(weights.reshape(D, nb, K), ((0, 0), (0, pb - nb), (0, 0))).reshape(N, K)
    spot = jnp.arange(N, dtype=jnp.int32)
    wf = jnp.where(
        place[:, :, None] == spot[None, None, :], factor[:, :, None], 0.0
    ).astype(BF16).reshape(N, K * N)
    place_t, factor_t = place.T.reshape(1, K * N), factor.T.reshape(1, K * N)
    wg = jnp.where(place_t == spot[:, None], factor_t, 0.0).astype(BF16)
    cf = coupling[0].transpose(2, 0, 1).reshape(B, K * B)
    cg = coupling[0].transpose(1, 0, 2).reshape(B, K * B)

    dims = (S, D, R, nb, pb, B, K, 1.0 / math.sqrt(NB * B * S))
    panel_buf = (D, R, pb, B)
    vm = pl.BlockSpec(memory_space=pltpu.VMEM)
    tangent, adjoint, proj = pl.pallas_call(
        functools.partial(kernel, dims),
        out_shape=(
            jax.ShapeDtypeStruct(panel_buf, BF16),
            jax.ShapeDtypeStruct(panel_buf, BF16),
            jax.ShapeDtypeStruct((R, 128), F32),
        ),
        in_specs=[vm] * 7 + [pl.BlockSpec(memory_space=pltpu.SMEM)],
        out_specs=(vm, vm, vm),
        scratch_shapes=[pltpu.VMEM((EXCHANGES,) + panel_buf, BF16)]
        + [pltpu.VMEM(panel_buf, BF16)] * 8
        + [
            pltpu.VMEM((rows * pb, B), F32),
            pltpu.VMEM((rows * pb, B), F32),
            pltpu.VMEM((rows, 128), F32),
            pltpu.VMEM((D, rows, 128), F32),
            pltpu.VMEM((rows, 128), F32),
            pltpu.VMEM((S, rows, 128), F32),
            pltpu.SemaphoreType.DMA((EXCHANGES, D)),
            pltpu.SemaphoreType.DMA((EXCHANGES, D)),
            pltpu.SemaphoreType.DMA((D,)),
            pltpu.SemaphoreType.DMA((D,)),
            pltpu.SemaphoreType.DMA((S,)),
            pltpu.SemaphoreType.DMA((S,)),
        ],
        compiler_params=pltpu.CompilerParams(
            collective_id=0, has_side_effects=True, vmem_limit_bytes=48 * 2**20
        ),
    )(padded(panel), padded(seeds[0]), inverses[0], cf, cg, wf, wg, counts)
    return flat(tangent)[None], flat(adjoint)[None], proj[:, :rows]


def solution(mesh):
    in_specs = (
        P("dir", None),
        P("seg", "dir", None),
        P("seg", "dir", None, None),
        P("seg", None, None, None),
        P(),
        P(),
        P(),
    )
    out_specs = (P("seg", "dir", None), P("seg", "dir", None), P("dir", None))
    return jax.shard_map(body, mesh=mesh, in_specs=in_specs, out_specs=out_specs, check_vma=False)
```

time: 723 us -> 158 us (0.22)
  other arithmetic: 325 us -> 1.18 us
  waiting for transfers between devices: 148 us -> 0 us
  Pallas kernels: 0 us -> 138 us
  matrix products: 123 us -> 0 us
  starting transfers between devices: 36.8 us -> 0 us
  local copies, waits for them, and re-layouts: 47 us -> 17.9 us
  blocking collectives: 25.7 us -> 0 us
  between operations: 16.2 us -> 0.78 us
    scatter-add x8 -> x0, other arithmetic: 306 us -> none  [couple_adjoint(): spread = jnp.zeros(reached.shape, jnp.float32).at[:, pattern, :].add(terms)]
    pallas_call x0 -> x1, Pallas kernels: none -> 138 us  [body(): pl.pallas_call(functools.partial(kernel, dims), out_shape=(jax.ShapeDtype...]
    dot_general x33 -> x0, matrix products: 123 us -> none  [the longest x8 70.7 us: forward_blocks(): jnp.einsum('ieq,riq->rie', inverse_table, current, preferred_element_type...]
    all_gather x1 -> x0, waiting for transfers between devices: 110 us -> none  [body(): inverse_all = lax.all_gather(inverse_local, 'dir', axis=0, tiled=True)]
    gather x8 -> x0, local copies, waits for them, and re-layouts: 34.4 us -> none  [couple_forward(): picked = current[:, pattern, :]]
    ppermute x8 -> x0, waiting for transfers between devices: 30.8 us -> none  [the longest x4 17.4 us: shifted_2(): return lax.ppermute(value, axis, pairs)]
    ppermute x8 -> x0, starting transfers between devices: 28.6 us -> none  [the longest x4 17.4 us: shifted(): return lax.ppermute(array, axis, pairs)]
    unnamed x1 -> x0, blocking collectives: 14.8 us -> none
  transfers between devices with their start and end apart: 11 -> 0, of which waited for: 10 -> 0; matrix products, arithmetic and copies ran while one was open for 52% -> 0% of each run, Pallas kernels for 0% -> 0%
where the time goes in v1:
time: 158 us; the launch traced here: 157 us
  Pallas kernels  138 us (87%)
  local copies, waits for them, and re-layouts  17.9 us (11%)
    pallas_call x1, Pallas kernels, body(): pl.pallas_call(functools.partial(kernel, dims), out_shape=(jax.ShapeDtype...  138 us
    eq x5, local copies, waits for them, and re-layouts, body(): place[:, :, None] == spot[None, None, :]  3.51 us

profile of v1, /device:TPU:0, one launch (start us, length us, event | category | flops | bytes accessed | tf_op | source)
XLA Modules:
  0.0 157.4 jit_solution(14023432060902994802)
XLA Ops:
  0.6 0.7 fusion
  1.3 0.1 reshape.36
  1.4 0.1 eq.39
  1.5 1.4 eq.40
  2.9 0.0 copy-start.6
  2.9 2.1 %copy.17 = s32[384,1152]{1,0:T(8,128)S(1)} copy(s32[384,1152]{0,1:T(8,128)} %bitcast.34) | data formatting | bytes 3538944 | tf_op jit(solution)/shard_map/eq | solution.py:303
  4.9 0.0 copy-done.6
  4.9 0.1 reshape.37
  5.0 0.1 broadcast_in_dim.30
  5.1 0.0 copy-start.5
  5.2 0.1 broadcast_in_dim.31
  5.2 0.5 copy-done.5
  5.7 0.9 copy.18
  6.6 0.2 select_convert_fusion.1.wf_ref
  6.8 0.0 copy-start.4
  6.9 0.7 broadcast_in_dim.34
  7.6 0.0 copy-start
  7.6 0.0 copy-start.3
  7.6 0.3 select_convert_fusion.wg_ref
  7.9 1.2 reshape.33
  9.1 1.7 %reshape_squeeze.3 = bf16[2,8,44,128]{3,2,1,0:T(8,128)(2,1)} reshape(bf16[1,2,45056]{2,1,0:T(2,128)(2,1)} %param.8) | data formatting | bytes 360448 | tf_op jit(solution)/shard_map/reshape;squeeze | solution.py:291
  10.9 0.9 copy.25
  11.8 0.7 pad.16.seeds_ref
  12.5 0.0 copy-done.4
  12.5 0.8 copy.16
  13.2 1.0 copy.20.cg_ref
  14.3 1.6 %copy.19.cf_ref = bf16[128,384]{1,0:T(8,128)(2,1)} copy(bf16[128,384]{0,1:T(8,128)(2,1)} %bitcast.38) | data formatting | bytes 196608 | tf_op jit(solution)/shard_map/reshape | solution.py:307
  15.9 0.0 copy-done
  15.9 0.0 copy-done.3
  15.9 0.0 copy-start.1
  15.9 0.9 copy-done.1
  16.8 0.0 copy-start.2
  16.8 0.9 copy-done.2
  17.7 137.5 %shard_map.94 = (bf16[8,2,48,128]{3,2,1,0:T(8,128)(2,1)S(1)}, bf16[8,2,48,128]{3,2,1,0:T(8,128)(2,1)S(1)}, f32[2,128]{1,0:T(2,128)S(1)}) custom-call(bf16[8,2,48,128]{3,2,1,0:T(8,128)(2,1)S(1)} %pad.15.panel_ref, bf16[8,2,48,128]{3,2,1,0:T(8,128)(2,1)S(1)} %copy-done.1, bf16[44,128,128]{2,1,0:T(8,128)(2,1)S(1)} %bitcast.32, bf16[128,384]{1,0:T(8,128)(2,1)S(1)} %copy-done.2, ...), custom_call_target="tpu_custom_call" | custom-call | tf_op jit(solution)/shard_map/pallas_call | solution.py:313
  155.3 0.7 broadcast_in_dim_reshape.8
  156.1 0.7 broadcast_in_dim_reshape.9
  156.8 0.6 copy.28
  (10 shorter events, 0.1 us)
Async XLA Ops:
  2.9 2.1 %copy-start.6 = (f32[352,3]{0,1:T(4,128)S(1)}, f32[352,3]{0,1:T(4,128)}, u32[]{:S(2)}) copy-start(f32[352,3]{0,1:T(4,128)} %param.11) | copy-start | bytes 12676
  5.1 0.6 copy-start.5
  6.8 5.7 %copy-start.4 = (bf16[1,3,128,128]{3,2,1,0:T(8,128)(2,1)S(1)}, bf16[1,3,128,128]{3,2,1,0:T(8,128)(2,1)}, u32[]{:S(2)}) copy-start(bf16[1,3,128,128]{3,2,1,0:T(8,128)(2,1)} %param.10) | copy-start | bytes 294916
  7.6 8.3 %copy-start = (bf16[1,44,128,128]{3,2,1,0:T(8,128)(2,1)S(1)}, bf16[1,44,128,128]{3,2,1,0:T(8,128)(2,1)}, u32[]{:S(2)}) copy-start(bf16[1,44,128,128]{3,2,1,0:T(8,128)(2,1)} %param.9) | copy-start | bytes 4325380
  7.6 8.3 %copy-start.3 = (s32[4]{0:T(128)S(1)}, s32[4]{0:T(128)}, u32[]{:S(2)}) copy-start(s32[4]{0:T(128)} %counts_ref.1) | copy-start | bytes 52
  15.9 0.9 copy-start.1
  16.8 0.9 copy-start.2

commit v2 on v1

v2 whole, which is shorter than its diff:
```python
import functools
import math

import jax
import jax.numpy as jnp
from jax import lax
from jax.experimental import pallas as pl
from jax.experimental.pallas import tpu as pltpu
from jax.sharding import PartitionSpec as P

MESH = pl.DeviceIdType.MESH
F32 = jnp.float32
BF16 = jnp.bfloat16

SEED, F1, F2, F3, TAN, HAND_F, HAND_G, G2, G3, G4, ADJ = range(11)
EXCHANGES = 11


def kernel(
    dims,
    panel_ref, seeds_ref, inv_ref, coup_ref, pat_ref, wts_ref, counts_ref,
    tangent_ref, adjoint_ref, proj_ref,
    land, f1s, f2s, f3s, tans, g2s, g3s, g4s, adjs, wf, wg, ubuf, obuf, pbuf, rp, qbuf, rq,
    send_sem, recv_sem, ps_sem, pr_sem, qs_sem, qr_sem,
):
    S, D, R, NG, nb, pb, B, K, scale = dims
    RG = R // NG
    N = D * pb
    rows = D * RG
    dirs = D * R
    s = lax.axis_index("seg")
    d = lax.axis_index("dir")
    tangent_first = s < lax.rem(1 - s + S, S)
    groups = range(NG)

    def partner(x):
        if D & (D - 1):
            return lax.rem(d + x, D)
        to, bit = d, 1
        while bit < D:
            if x & bit:
                to = to + bit * (1 - 2 * lax.rem(lax.div(d, bit), 2))
            bit *= 2
        return to

    def source(x):
        return lax.rem(d + D - x, D) if D & (D - 1) else partner(x)

    others = range(D - 1, 0, -1)

    barrier = pltpu.get_barrier_semaphore()
    total = S * D
    lin = s * D + d

    def greet(o, c):
        t = lax.rem(lin + o, total)
        pl.semaphore_signal(
            barrier, inc=1, device_id=(lax.div(t, D), lax.rem(t, D)), device_id_type=MESH
        )
        return c

    lax.fori_loop(1, total, greet, 0)

    spot = lax.broadcasted_iota(jnp.int32, (N, N), 1)

    def forward_matrix():
        for k in range(K):
            wf[:, k * N : (k + 1) * N] = jnp.where(
                pat_ref[:, k : k + 1] == spot, wts_ref[:, k : k + 1], 0.0
            ).astype(BF16)

    def adjoint_matrix():
        for k in range(K):
            wg[:, k * N : (k + 1) * N] = jnp.where(
                pat_ref[:, k : k + 1] == spot, wts_ref[:, k : k + 1], 0.0
            ).T.astype(BF16)

    @pl.when(tangent_first)
    def _():
        forward_matrix()

    obuf[...] = jnp.zeros_like(obuf)
    pl.semaphore_wait(barrier, total - 1)

    def copy(src, ex, g, seg, to, came_from):
        return pltpu.make_async_remote_copy(
            src_ref=src.at[g, to],
            dst_ref=land.at[ex, g, came_from],
            send_sem=send_sem.at[ex, g, to],
            recv_sem=recv_sem.at[ex, g, came_from],
            device_id=(seg, to),
            device_id_type=MESH,
        )

    def send_group(src, ex, g):
        for x in others:
            copy(src, ex, g, s, partner(x), d).start()
        land[ex, g, d] = src[g, d]

    def wait_group(src, ex, g):
        for x in others:
            j = source(x)
            copy(src, ex, g, s, j, j).wait_recv()

    def sent_group(src, ex):
        def one(o, c):
            for g in groups:
                copy(src, ex, g, s, lax.rem(d + o, D), d).wait_send()
            return c

        lax.fori_loop(1, D, one, 0)

    def send_on(src, ex, g, seg):
        for x in list(others) + [0]:
            copy(src, ex, g, seg, partner(x), d).start()

    def wait_on(src, ex, g, seg):
        for j in range(D):
            copy(src, ex, g, seg, j, j).wait_recv()

    def sent_on(src, ex, seg):
        def one(o, c):
            for g in groups:
                copy(src, ex, g, seg, o, d).wait_send()
            return c

        lax.fori_loop(0, D, one, 0)

    def couple(value, w_ref, contract):
        x = [value[:, r].reshape(N, B) for r in range(RG)]
        rhs = jnp.concatenate(
            [
                jnp.concatenate(
                    [
                        lax.dot_general(
                            v, coup_ref[k], (((1,), (contract,)), ((), ())),
                            preferred_element_type=F32,
                        ).astype(BF16)
                        for v in x
                    ],
                    axis=1,
                )
                for k in range(K)
            ],
            axis=0,
        )
        acc = jnp.dot(w_ref[...], rhs, preferred_element_type=F32)
        out = [x[r].astype(F32) + acc[:, r * B : (r + 1) * B] for r in range(RG)]
        return [v.astype(BF16).reshape(D, pb, B) for v in out]

    def put(ref, g, parts):
        for r in range(RG):
            ref[g, :, r] = parts[r]

    batch = max(n for n in range(1, 17) if nb % n == 0)

    def invert(value, contract):
        ubuf[...] = value.astype(F32).reshape(rows * pb, B)

        def step(i, c):
            for u in range(batch):
                at = pl.ds(i * batch + u, rows, stride=pb)
                obuf[at, :] = lax.dot_general(
                    ubuf[at, :].astype(BF16),
                    inv_ref[i * batch + u],
                    (((1,), (contract,)), ((), ())),
                    preferred_element_type=F32,
                )
            return c

        lax.fori_loop(0, nb // batch, step, 0)
        return obuf[...].astype(BF16).reshape(D, RG, pb, B)

    more = counts_ref[s] > 1

    def tangent_round():
        for g in groups:
            @pl.when(s > 0)
            def _():
                wait_on(tans, HAND_F, g, s)

            first = jnp.where(s > 0, land[HAND_F, g], panel_ref[g])
            put(f1s, g, couple(first, wf, 1))
            send_group(f1s, F1, g)

        @pl.when(tangent_first)
        def _():
            for g in groups:
                send_group(seeds_ref, SEED, g)
            adjoint_matrix()

        for g in groups:
            wait_group(f1s, F1, g)
            f2s[g] = invert(land[F1, g], 1)
            send_group(f2s, F2, g)
        for g in groups:
            wait_group(f2s, F2, g)
            put(f3s, g, couple(land[F2, g], wf, 1))
            send_group(f3s, F3, g)
        for g in groups:
            wait_group(f3s, F3, g)
            tans[g] = jnp.where(more, invert(land[F3, g], 1), f2s[g])

            @pl.when(s < S - 1)
            def _():
                send_on(tans, HAND_F, g, lax.rem(s + 1, S))

        for g in groups:
            send_group(tans, TAN, g)

    def adjoint_round():
        @pl.when(jnp.logical_not(tangent_first))
        def _():
            for g in groups:
                send_group(seeds_ref, SEED, g)

        @pl.when(jnp.logical_not(tangent_first))
        def _():
            adjoint_matrix()
            forward_matrix()

        for g in groups:
            wait_group(seeds_ref, SEED, g)

            @pl.when(s != 1)
            def _():
                wait_on(adjs, HAND_G, g, s)

            entry = jnp.where(
                s != 1,
                (land[SEED, g].astype(F32) + land[HAND_G, g].astype(F32)).astype(BF16),
                land[SEED, g],
            )
            g2s[g] = invert(entry, 0)
            send_group(g2s, G2, g)
        for g in groups:
            wait_group(g2s, G2, g)
            put(g3s, g, couple(land[G2, g], wg, 0))
            send_group(g3s, G3, g)
        for g in groups:
            wait_group(g3s, G3, g)
            g4s[g] = invert(land[G3, g], 0)
            send_group(g4s, G4, g)
        for g in groups:
            wait_group(g4s, G4, g)
            last = couple(land[G4, g], wg, 0)
            put(adjs, g, [jnp.where(more, last[r], g3s[g, :, r]) for r in range(RG)])

            @pl.when(s != 2)
            def _():
                send_on(adjs, HAND_G, g, lax.rem(s + S - 1, S))

        for g in groups:
            send_group(adjs, ADJ, g)

    def turn(slot, c):
        now = (slot == 0) == tangent_first

        @pl.when(now)
        def _():
            tangent_round()

        @pl.when(jnp.logical_not(now))
        def _():
            adjoint_round()

        return c

    lax.fori_loop(0, 2, turn, 0)

    for g in groups:
        for r in range(RG):
            adjoint_ref[:, g * RG + r] = adjs[g, :, r]

    pbuf[...] = jnp.zeros_like(pbuf)

    def gathered(buf, i):
        return jnp.concatenate(
            [buf[pl.ds(i * batch + u, rows, stride=pb), :].astype(BF16) for u in range(batch)],
            axis=1,
        )

    for g in groups:
        wait_group(adjs, ADJ, g)
        ubuf[...] = land[ADJ, g].astype(F32).reshape(rows * pb, B)
        for h in groups:
            obuf[...] = tans[h].astype(F32).reshape(rows * pb, B)

            def gram(i, acc):
                return acc + lax.dot_general(
                    gathered(ubuf, i), gathered(obuf, i), (((1,), (1,)), ((), ())),
                    preferred_element_type=F32,
                )

            pbuf[g * rows : (g + 1) * rows, h * rows : (h + 1) * rows] = lax.fori_loop(
                0, nb // batch, gram, jnp.zeros((rows, rows), F32)
            )

    def pcopy(to, came_from):
        return pltpu.make_async_remote_copy(
            src_ref=pbuf, dst_ref=rp.at[came_from], send_sem=ps_sem.at[to],
            recv_sem=pr_sem.at[came_from], device_id=(s, to), device_id_type=MESH,
        )

    def qcopy(to, came_from):
        return pltpu.make_async_remote_copy(
            src_ref=qbuf, dst_ref=rq.at[came_from], send_sem=qs_sem.at[to],
            recv_sem=qr_sem.at[came_from], device_id=(to, d), device_id_type=MESH,
        )

    for x in others:
        pcopy(partner(x), d).start()
    rp[d] = pbuf[...]
    for x in others:
        j = source(x)
        pcopy(j, j).wait_recv()
    qbuf[...] = jnp.sum(rp[...], axis=0)
    for o in range(1, S):
        qcopy(lax.rem(s + o, S), s).start()
    rq[s] = qbuf[...]
    for g in groups:
        wait_group(tans, TAN, g)
        for r in range(RG):
            tangent_ref[:, g * RG + r] = land[TAN, g, :, r]
    for x in others:
        pcopy(partner(x), d).wait_send()
    for src, ex in (
        (seeds_ref, SEED), (f1s, F1), (f2s, F2), (f3s, F3), (tans, TAN),
        (g2s, G2), (g3s, G3), (g4s, G4), (adjs, ADJ),
    ):
        sent_group(src, ex)

    @pl.when(s < S - 1)
    def _():
        sent_on(tans, HAND_F, lax.rem(s + 1, S))

    @pl.when(s != 2)
    def _():
        sent_on(adjs, HAND_G, lax.rem(s + S - 1, S))

    for o in range(1, S):
        j = lax.rem(s + S - o, S)
        qcopy(j, j).wait_recv()
    pbuf[...] = jnp.sum(rq[...], axis=0) * scale
    for g in groups:
        proj_ref[g * RG : (g + 1) * RG, :] = pbuf[pl.ds(g * rows + d * RG, RG), :]
    for o in range(1, S):
        qcopy(lax.rem(s + o, S), s).wait_send()


def body(panel, seeds, inverses, coupling, weights, pattern, counts):
    NB, K = pattern.shape
    B = coupling.shape[-1]
    R = panel.shape[0]
    S, D = lax.axis_size("seg"), lax.axis_size("dir")
    nb = NB // D
    pb = -(-nb // 16) * 16
    N = D * pb
    NG = 2 if R % 2 == 0 else 1
    RG = R // NG
    rows, dirs = D * RG, D * R

    def padded(flat):
        cut = flat.reshape(NG, RG, D, nb, B).transpose(0, 2, 1, 3, 4)
        return jnp.pad(cut, ((0, 0),) * 3 + ((0, pb - nb), (0, 0)))

    def flat(cut):
        return cut[:, :, :nb].transpose(1, 0, 2, 3).reshape(R, NB * B)

    place = (pattern // nb) * pb + pattern % nb
    gap = ((0, 0), (0, pb - nb), (0, 0))
    place = jnp.pad(place.reshape(D, nb, K), gap, constant_values=-1).reshape(N, K)
    factor = jnp.pad(weights.reshape(D, nb, K), gap).reshape(N, K)

    dims = (S, D, R, NG, nb, pb, B, K, 1.0 / math.sqrt(NB * B * S))
    panel_buf = (NG, D, RG, pb, B)
    vm = pl.BlockSpec(memory_space=pltpu.VMEM)
    tangent, adjoint, proj = pl.pallas_call(
        functools.partial(kernel, dims),
        out_shape=(
            jax.ShapeDtypeStruct((D, R, pb, B), BF16),
            jax.ShapeDtypeStruct((D, R, pb, B), BF16),
            jax.ShapeDtypeStruct((R, 128), F32),
        ),
        in_specs=[vm] * 6 + [pl.BlockSpec(memory_space=pltpu.SMEM)],
        out_specs=(vm, vm, vm),
        scratch_shapes=[pltpu.VMEM((EXCHANGES,) + panel_buf, BF16)]
        + [pltpu.VMEM(panel_buf, BF16)] * 8
        + [
            pltpu.VMEM((N, K * N), BF16),
            pltpu.VMEM((N, K * N), BF16),
            pltpu.VMEM((rows * pb, B), F32),
            pltpu.VMEM((rows * pb, B), F32),
            pltpu.VMEM((dirs, 128), F32),
            pltpu.VMEM((D, dirs, 128), F32),
            pltpu.VMEM((dirs, 128), F32),
            pltpu.VMEM((S, dirs, 128), F32),
            pltpu.SemaphoreType.DMA((EXCHANGES, NG, D)),
            pltpu.SemaphoreType.DMA((EXCHANGES, NG, D)),
            pltpu.SemaphoreType.DMA((D,)),
            pltpu.SemaphoreType.DMA((D,)),
            pltpu.SemaphoreType.DMA((S,)),
            pltpu.SemaphoreType.DMA((S,)),
        ],
        compiler_params=pltpu.CompilerParams(
            collective_id=0, has_side_effects=True, vmem_limit_bytes=48 * 2**20
        ),
    )(padded(panel), padded(seeds[0]), inverses[0], coupling[0], place, factor, counts)
    ordered = proj[:, :dirs].reshape(R, NG, D, RG).transpose(0, 2, 1, 3).reshape(R, dirs)
    return flat(tangent)[None], flat(adjoint)[None], ordered


def solution(mesh):
    in_specs = (
        P("dir", None),
        P("seg", "dir", None),
        P("seg", "dir", None, None),
        P("seg", None, None, None),
        P(),
        P(),
        P(),
    )
    out_specs = (P("seg", "dir", None), P("seg", "dir", None), P("dir", None))
    return jax.shard_map(body, mesh=mesh, in_specs=in_specs, out_specs=out_specs, check_vma=False)
```

time: 158 us -> 132 us (0.84)
  local copies, waits for them, and re-layouts: 17.9 us -> 4.84 us
  Pallas kernels: 138 us -> 125 us
    pallas_call x1, Pallas kernels: 138 us -> 125 us  [body(): pl.pallas_call(functools.partial(kernel, dims), out_shape=(jax.ShapeDtype...]
    eq x6 -> x0, local copies, waits for them, and re-layouts: 3.52 us -> none  [the longest x5 3.51 us: body(): place[:, :, None] == spot[None, None, :]]
    unnamed x15 -> x8, local copies, waits for them, and re-layouts: 2.88 us -> 0.02 us
    reshape x5 -> x4, local copies, waits for them, and re-layouts: 3.95 us -> 1.66 us  [the longest x2 0.93 us: body(): factor = jnp.pad(weights.reshape(D, nb, K), gap).reshape(N, K)]
    broadcast_in_dim x4 -> x0, local copies, waits for them, and re-layouts: 1.76 us -> none  [the longest x3 1.03 us: body(): jnp.where(place[:, :, None] == spot[None, None, :], factor[:, :, None], 0.0)]
where the time goes in v2:
time: 132 us
  Pallas kernels  125 us (95%)
  local copies, waits for them, and re-layouts  4.84 us (4%)
    pallas_call x1, Pallas kernels, body(): pl.pallas_call(functools.partial(kernel, dims), out_shape=(jax.ShapeDtype...  125 us

profile of v2, /device:TPU:0, one launch (start us, length us, event | category | flops | bytes accessed | tf_op | source)
XLA Modules:
  0.0 131.8 jit_solution(16713312859343918066)
XLA Ops:
  0.6 0.0 copy-start.2
  0.6 0.0 copy-start.1
  0.7 0.0 copy-start
  0.7 0.0 copy-start.3
  0.7 0.8 fusion
  1.5 0.1 reshape.24
  1.6 0.8 reshape.26
  2.4 0.2 copy.16
  2.6 0.2 copy.15
  2.8 1.1 transpose_reshape.3
  3.9 0.0 copy-done.3
  3.9 0.1 transpose_reshape_squeeze.3
  4.1 0.0 copy-done.2
  4.1 0.0 copy-done.1
  4.1 0.0 copy-done
  4.1 125.4 %shard_map.94 = (bf16[8,2,48,128]{3,2,1,0:T(8,128)(2,1)S(1)}, bf16[8,2,48,128]{3,2,1,0:T(8,128)(2,1)S(1)}, f32[2,128]{1,0:T(2,128)S(1)}) custom-call(bf16[2,8,1,48,128]{4,3,2,1,0:T(8,128)(2,1)S(1)} %pad.15.panel_ref, bf16[2,8,1,48,128]{4,3,2,1,0:T(8,128)(2,1)S(1)} %pad.16.seeds_ref, bf16[44,128,128]{2,1,0:T(8,128)(2,1)S(1)} %bitcast.20, ...), custom_call_target="tpu_custom_call" | custom-call | tf_op jit(solution)/shard_map/pallas_call | solution.py:378
  129.5 0.7 broadcast_in_dim_reshape.7
  130.3 0.1 reshape.28
  130.4 0.1 copy.19
  130.4 0.6 reshape.29
  131.1 0.7 broadcast_in_dim_reshape.6
  (7 shorter events, 0.2 us)
Async XLA Ops:
  0.6 3.4 %copy-start.2 = (s32[4]{0:T(128)S(1)}, s32[4]{0:T(128)}, u32[]{:S(2)}) copy-start(s32[4]{0:T(128)} %counts_ref.1) | copy-start | bytes 52
  0.6 3.4 %copy-start.1 = (bf16[1,3,128,128]{3,2,1,0:T(8,128)(2,1)S(1)}, bf16[1,3,128,128]{3,2,1,0:T(8,128)(2,1)}, u32[]{:S(2)}) copy-start(bf16[1,3,128,128]{3,2,1,0:T(8,128)(2,1)} %param.10) | copy-start | bytes 294916
  0.7 3.4 %copy-start = (bf16[1,44,128,128]{3,2,1,0:T(8,128)(2,1)S(1)}, bf16[1,44,128,128]{3,2,1,0:T(8,128)(2,1)}, u32[]{:S(2)}) copy-start(bf16[1,44,128,128]{3,2,1,0:T(8,128)(2,1)} %param.9) | copy-start | bytes 4325380
  0.7 3.2 %copy-start.3 = (bf16[1,2,45056]{2,1,0:T(2,128)(2,1)S(1)}, bf16[1,2,45056]{2,1,0:T(2,128)(2,1)}, u32[]{:S(2)}) copy-start(bf16[1,2,45056]{2,1,0:T(2,128)(2,1)} %param.8) | copy-start | bytes 540676

commit v3 on v2

--- a/solution.py
+++ b/solution.py
@@ -125,6 +125,16 @@
             return c
 
         lax.fori_loop(0, D, one, 0)
+
+    def give_back(arrived, ex, g, seg):
+        return pltpu.make_async_remote_copy(
+            src_ref=land.at[arrived, g],
+            dst_ref=land.at[ex, g],
+            send_sem=send_sem.at[ex, g, d],
+            recv_sem=recv_sem.at[ex, g, d],
+            device_id=(seg, d),
+            device_id_type=MESH,
+        )
 
     def couple(value, w_ref, contract):
         x = [value[:, r].reshape(N, B) for r in range(RG)]
@@ -152,7 +162,7 @@
         for r in range(RG):
             ref[g, :, r] = parts[r]
 
-    batch = max(n for n in range(1, 17) if nb % n == 0)
+    batch = max(n for n in range(1, 65) if nb % n == 0)
 
     def invert(value, contract):
         ubuf[...] = value.astype(F32).reshape(rows * pb, B)
@@ -183,20 +193,33 @@
             put(f1s, g, couple(first, wf, 1))
             send_group(f1s, F1, g)
 
+            @pl.when(s > 0)
+            def _():
+                give_back(HAND_F, TAN, g, s - 1).start()
+
         @pl.when(tangent_first)
         def _():
-            for g in groups:
-                send_group(seeds_ref, SEED, g)
             adjoint_matrix()
 
         for g in groups:
             wait_group(f1s, F1, g)
             f2s[g] = invert(land[F1, g], 1)
             send_group(f2s, F2, g)
+
+        @pl.when(s == 0)
+        def _():
+            send_group(seeds_ref, SEED, 0)
+
         for g in groups:
             wait_group(f2s, F2, g)
             put(f3s, g, couple(land[F2, g], wf, 1))
             send_group(f3s, F3, g)
+
+        @pl.when(s == 0)
+        def _():
+            for g in groups[1:]:
+                send_group(seeds_ref, SEED, g)
+
         for g in groups:
             wait_group(f3s, F3, g)
             tans[g] = jnp.where(more, invert(land[F3, g], 1), f2s[g])
@@ -205,20 +228,11 @@
             def _():
                 send_on(tans, HAND_F, g, lax.rem(s + 1, S))
 
-        for g in groups:
-            send_group(tans, TAN, g)
+            @pl.when(s == S - 1)
+            def _():
+                send_group(tans, TAN, g)
 
     def adjoint_round():
-        @pl.when(jnp.logical_not(tangent_first))
-        def _():
-            for g in groups:
-                send_group(seeds_ref, SEED, g)
-
-        @pl.when(jnp.logical_not(tangent_first))
-        def _():
-            adjoint_matrix()
-            forward_matrix()
-
         for g in groups:
             wait_group(seeds_ref, SEED, g)
 
@@ -233,10 +247,24 @@
             )
             g2s[g] = invert(entry, 0)
             send_group(g2s, G2, g)
+
+            @pl.when(s != 1)
+            def _():
+                give_back(HAND_G, ADJ, g, lax.rem(s + 1, S)).start()
+
+        @pl.when(jnp.logical_not(tangent_first))
+        def _():
+            adjoint_matrix()
+
         for g in groups:
             wait_group(g2s, G2, g)
             put(g3s, g, couple(land[G2, g], wg, 0))
             send_group(g3s, G3, g)
+
+        @pl.when(jnp.logical_not(tangent_first))
+        def _():
+            forward_matrix()
+
         for g in groups:
             wait_group(g3s, G3, g)
             g4s[g] = invert(land[G3, g], 0)
@@ -250,8 +278,9 @@
             def _():
                 send_on(adjs, HAND_G, g, lax.rem(s + S - 1, S))
 
-        for g in groups:
-            send_group(adjs, ADJ, g)
+            @pl.when(s == 2)
+            def _():
+                send_group(adjs, ADJ, g)
 
     def turn(slot, c):
         now = (slot == 0) == tangent_first
@@ -265,6 +294,11 @@
             adjoint_round()
 
         return c
+
+    @pl.when(s != 0)
+    def _():
+        for g in groups:
+            send_group(seeds_ref, SEED, g)
 
     lax.fori_loop(0, 2, turn, 0)
 
@@ -281,7 +315,14 @@
         )
 
     for g in groups:
-        wait_group(adjs, ADJ, g)
+        @pl.when(s == 2)
+        def _():
+            wait_group(adjs, ADJ, g)
+
+        @pl.when(s != 2)
+        def _():
+            give_back(HAND_G, ADJ, g, s).wait_recv()
+
         ubuf[...] = land[ADJ, g].astype(F32).reshape(rows * pb, B)
         for h in groups:
             obuf[...] = tans[h].astype(F32).reshape(rows * pb, B)
@@ -319,14 +360,21 @@
         qcopy(lax.rem(s + o, S), s).start()
     rq[s] = qbuf[...]
     for g in groups:
-        wait_group(tans, TAN, g)
+        @pl.when(s == S - 1)
+        def _():
+            wait_group(tans, TAN, g)
+
+        @pl.when(s < S - 1)
+        def _():
+            give_back(HAND_F, TAN, g, s).wait_recv()
+
         for r in range(RG):
             tangent_ref[:, g * RG + r] = land[TAN, g, :, r]
     for x in others:
         pcopy(partner(x), d).wait_send()
     for src, ex in (
-        (seeds_ref, SEED), (f1s, F1), (f2s, F2), (f3s, F3), (tans, TAN),
-        (g2s, G2), (g3s, G3), (g4s, G4), (adjs, ADJ),
+        (seeds_ref, SEED), (f1s, F1), (f2s, F2), (f3s, F3),
+        (g2s, G2), (g3s, G3), (g4s, G4),
     ):
         sent_group(src, ex)
 
@@ -334,9 +382,27 @@
     def _():
         sent_on(tans, HAND_F, lax.rem(s + 1, S))
 
+    @pl.when(s == S - 1)
+    def _():
+        sent_group(tans, TAN)
+
+    @pl.when(s > 0)
+    def _():
+        for g in groups:
+            give_back(HAND_F, TAN, g, s - 1).wait_send()
+
     @pl.when(s != 2)
     def _():
         sent_on(adjs, HAND_G, lax.rem(s + S - 1, S))
+
+    @pl.when(s == 2)
+    def _():
+        sent_group(adjs, ADJ)
+
+    @pl.when(s != 1)
+    def _():
+        for g in groups:
+            give_back(HAND_G, ADJ, g, lax.rem(s + 1, S)).wait_send()
 
     for o in range(1, S):
         j = lax.rem(s + S - o, S)

time: 132 us -> 117 us (0.89)
  Pallas kernels: 125 us -> 110 us
    pallas_call x1, Pallas kernels: 125 us -> 110 us  [body(): pl.pallas_call(functools.partial(kernel, dims), out_shape=(jax.ShapeDtype...]
where the time goes in v3:
time: 117 us
  Pallas kernels  110 us (94%)
  local copies, waits for them, and re-layouts  4.84 us (4%)
    pallas_call x1, Pallas kernels, body(): pl.pallas_call(functools.partial(kernel, dims), out_shape=(jax.ShapeDtype...  110 us

profile of v3, /device:TPU:0, one launch (start us, length us, event | category | flops | bytes accessed | tf_op | source)
XLA Modules:
  0.0 116.7 jit_solution(13409733237030152934)
XLA Ops:
  0.6 0.0 copy-start.2
  0.6 0.0 copy-start.1
  0.7 0.0 copy-start
  0.7 0.0 copy-start.3
  0.7 0.8 fusion
  1.5 0.1 reshape.24
  1.6 0.8 reshape.26
  2.4 0.2 copy.16
  2.6 0.2 copy.15
  2.8 1.1 transpose_reshape.3
  3.9 0.0 copy-done.3
  3.9 0.1 transpose_reshape_squeeze.3
  4.1 0.0 copy-done.2
  4.1 0.0 copy-done.1
  4.1 0.0 copy-done
  4.1 110.2 %shard_map.94 = (bf16[8,2,48,128]{3,2,1,0:T(8,128)(2,1)S(1)}, bf16[8,2,48,128]{3,2,1,0:T(8,128)(2,1)S(1)}, f32[2,128]{1,0:T(2,128)S(1)}) custom-call(bf16[2,8,1,48,128]{4,3,2,1,0:T(8,128)(2,1)S(1)} %pad.15.panel_ref, bf16[2,8,1,48,128]{4,3,2,1,0:T(8,128)(2,1)S(1)} %pad.16.seeds_ref, bf16[44,128,128]{2,1,0:T(8,128)(2,1)S(1)} %bitcast.20, ...), custom_call_target="tpu_custom_call" | custom-call | tf_op jit(solution)/shard_map/pallas_call | solution.py:444
  114.4 0.7 broadcast_in_dim_reshape.7
  115.1 0.1 reshape.28
  115.2 0.1 copy.19
  115.3 0.6 reshape.29
  116.0 0.7 broadcast_in_dim_reshape.6
  (7 shorter events, 0.2 us)
Async XLA Ops:
  0.6 3.4 %copy-start.2 = (s32[4]{0:T(128)S(1)}, s32[4]{0:T(128)}, u32[]{:S(2)}) copy-start(s32[4]{0:T(128)} %counts_ref.1) | copy-start | bytes 52
  0.6 3.4 %copy-start.1 = (bf16[1,3,128,128]{3,2,1,0:T(8,128)(2,1)S(1)}, bf16[1,3,128,128]{3,2,1,0:T(8,128)(2,1)}, u32[]{:S(2)}) copy-start(bf16[1,3,128,128]{3,2,1,0:T(8,128)(2,1)} %param.10) | copy-start | bytes 294916
  0.7 3.4 %copy-start = (bf16[1,44,128,128]{3,2,1,0:T(8,128)(2,1)S(1)}, bf16[1,44,128,128]{3,2,1,0:T(8,128)(2,1)}, u32[]{:S(2)}) copy-start(bf16[1,44,128,128]{3,2,1,0:T(8,128)(2,1)} %param.9) | copy-start | bytes 4325380
  0.7 3.2 %copy-start.3 = (bf16[1,2,45056]{2,1,0:T(2,128)(2,1)S(1)}, bf16[1,2,45056]{2,1,0:T(2,128)(2,1)}, u32[]{:S(2)}) copy-start(bf16[1,2,45056]{2,1,0:T(2,128)(2,1)} %param.8) | copy-start | bytes 540676
